TPU v7x, 512 devices: a whole 4x4x16 slice. The times are simulated.
512 devices in a mesh: wide: 32 (over z_lo, y, core), narrow: 16 (over x, z_hi).
Axes of the slice: x: 4, y: 4, z: 16 (z_hi: 4, z_lo: 4; z = z_hi * 4 + z_lo), core: 2. Of those that a mesh axis runs over, the one named last changes fastest.
Arguments:
- vectors: bfloat16 [3, 65536, 128], P(None, ('wide', 'narrow')), may hold values from -18 to 18
- hessian: bfloat16 [3, 3, 61, 65536], P(None, None, None, ('wide', 'narrow')), may hold values from -0.9 to 5.4
- neighbours: int32 [60, 65536], P(None, ('wide', 'narrow')), may hold values from 0 to 415
- halo_atoms: int32 [16384], P(('wide', 'narrow')), may hold values from 0 to 127
- labels: int32 [65536], P(('wide', 'narrow')), may hold values from 0 to 15
- masses: float32 [2, 16], replicated, may hold values from 1 to 32
- rotation: float32 [2, 128, 128], replicated, may hold values from -0.5 to 0.5
Outputs:
- gram: float32 [2, 128, 128], replicated
- rotated: bfloat16 [2, 3, 65536, 128], P(None, None, ('wide', 'narrow'))
Inputs may be any that keep to these rules, and one draw needn't show every extreme that they name: `neighbours`: A row below 128 is a local atom of the domain; a row r at or above it is boundary atom (r - 128) % 32 of block (r - 128) // 32 in the 3x3 order of the steps.
All inputs are finite; a program needn't handle non-finite values.
Results may differ from a plain program's by a relative error of at most 0.003.
Values may be sent and summed in bfloat16 or wider, within the bound.
A program may use at most 64 MiB of HBM per device.

v0:
```python
import jax
import jax.numpy as jnp
from jax import lax
from jax.sharding import PartitionSpec as P


def padded(array, sides, width):
    for axis, dim in sides:
        size, length = (lax.axis_size(axis), array.shape[dim])
        up = [(i, (i + 1) % size) for i in range(size - 1)]
        down = [(j, i) for i, j in up]
        last = lax.slice_in_dim(array, length - width, length, axis=dim)
        leading = lax.slice_in_dim(array, 0, width, axis=dim)
        before = lax.ppermute(last, axis, up)
        after = lax.ppermute(leading, axis, down)
        array = jnp.concatenate([before, array, after], axis=dim)
    return array


def class_factors(inverse_roots, classes):
    onehot = (
        classes[None, :] == jnp.arange(inverse_roots.shape[1], dtype=jnp.int32)[:, None]
    ).astype(jnp.float32)
    return jnp.dot(inverse_roots, onehot, precision=lax.Precision.HIGHEST)


def scale_rows(rows_full, factors):
    return jnp.concatenate(
        [rows_full * factors[0][None, :, None], rows_full * factors[1][None, :, None]], axis=2
    ).astype(jnp.bfloat16)


def local(vectors, hessian, neighbours, halo_atoms, labels, masses, rotation):
    atoms_here = vectors.shape[1]
    width = vectors.shape[2]
    boundary = halo_atoms.shape[0]
    inverse_roots = lax.rsqrt(masses)
    factors = class_factors(inverse_roots, labels)
    vector_complete = vectors.astype(jnp.float32)
    scaled = scale_rows(vector_complete, factors)
    outgoing = jnp.take(scaled, halo_atoms, axis=1)[:, None, None]
    rims = padded(outgoing, (("wide", 1), ("narrow", 2)), 1)
    rim_rows = rims.reshape(3, 9 * boundary, 2 * width)
    extended = jnp.concatenate([scaled, rim_rows], axis=1)
    total = jnp.einsum("ija,jac->iac", hessian[:, :, 0], scaled, preferred_element_type=jnp.float32)

    def add_group(group, running):
        blocks = lax.dynamic_slice_in_dim(hessian, 1 + group * 4, 4, 2)
        indices = lax.dynamic_slice_in_dim(neighbours, group * 4, 4, 0)
        picked = jnp.take(extended, indices.reshape(-1), axis=1).reshape(
            3, 4, atoms_here, 2 * width
        )
        return running + jnp.einsum(
            "ijka,jkac->iac", blocks, picked, preferred_element_type=jnp.float32
        )

    total = lax.fori_loop(0, neighbours.shape[0] // 4, add_group, total)
    hydrogen_image = total[:, :, :width] * factors[0][None, :, None]
    deuterium_image = total[:, :, width:] * factors[1][None, :, None]
    partial_gram = jnp.stack(
        [
            jnp.einsum(
                "eqv,eqh->vh", vector_complete, hydrogen_image, precision=lax.Precision.HIGHEST
            ),
            jnp.einsum(
                "eqv,eqh->vh", vector_complete, deuterium_image, precision=lax.Precision.HIGHEST
            ),
        ]
    )
    atoms_all = 3.0 * atoms_here * lax.axis_size("wide") * lax.axis_size("narrow")
    images = (hydrogen_image, deuterium_image)
    gram = lax.psum(partial_gram, ("wide", "narrow")) / atoms_all
    outputs = []
    for isotope_variant in range(2):
        fresh_block = images[isotope_variant] - jnp.einsum(
            "jyx,xs->jys", vector_complete, gram[isotope_variant], precision=lax.Precision.HIGHEST
        )
        outputs.append(
            jnp.einsum(
                "jyx,xs->jys",
                fresh_block,
                rotation[isotope_variant],
                precision=lax.Precision.HIGHEST,
            ).astype(jnp.bfloat16)
        )
    return (gram, jnp.stack(outputs))


def solution(mesh):
    return jax.shard_map(
        local,
        mesh=mesh,
        in_specs=(
            P(None, ("wide", "narrow"), None),
            P(None, None, None, ("wide", "narrow")),
            P(None, ("wide", "narrow")),
            P(("wide", "narrow")),
            P(("wide", "narrow")),
            P(),
            P(),
        ),
        out_specs=(P(), P(None, None, ("wide", "narrow"), None)),
        check_vma=False,
    )
```

profile of v0, /device:TPU:1, one launch (start us, length us, event | category | flops | bytes accessed | tf_op | source)
XLA Modules:
  0.0 598.3 jit_solution(16573963337587809548)
XLA Ops:
  11.3 8.8 %collective-permute-start.1 = (bf16[3,1,1,32,256]{4,0,3,2,1:T(4,128)(2,1)S(1)}, bf16[3,1,1,32,256]{4,0,3,2,1:T(4,128)(2,1)S(1)}, u32[]{:S(2)}, u32[]{:S(2)}) collective-permute-start(bf16[3,1,1,32,256]{4,0,3,2,1:T(4,128)(2,1)S(1)} %bitcast_select_fusion), channel_id=1, source_target_pairs={{16,0},{32,16},{48,32},{64,48},{80,64},{96,80},{112,96},{128,112},... | collective-permute-start | bytes 147464 | tf_op jit(solution)/shard_map/ppermute | solution.py:15
  20.1 1.9 collective-permute-start
  24.8 7.9 %collective-permute-start.2 = (bf16[3,3,1,32,256]{4,0,3,2,1:T(4,128)(2,1)S(1)}, bf16[3,3,1,32,256]{4,0,3,2,1:T(4,128)(2,1)S(1)}, u32[]{:S(2)}, u32[]{:S(2)}) collective-permute-start(bf16[3,3,1,32,256]{4,0,3,2,1:T(4,128)(2,1)S(1)} %pad_maximum_fusion.3), channel_id=1, source_target_pairs={{0,1},{1,2},{2,3},{3,4},{4,5},{5,6},{6,7},{7,8},{8,9},{9,10},{10,1... | collective-permute-start | bytes 442376 | tf_op jit(solution)/shard_map/ppermute | solution.py:14
  33.0 9.7 %collective-permute-done.3 = bf16[3,3,1,32,256]{4,0,3,2,1:T(4,128)(2,1)S(1)} collective-permute-done((bf16[3,3,1,32,256]{4,0,3,2,1:T(4,128)(2,1)S(1)}, bf16[3,3,1,32,256]{4,0,3,2,1:T(4,128)(2,1)S(1)}, u32[]{:S(2)}, u32[]{:S(2)}) %collective-permute-start.3) | collective-permute-done | bytes 147488 | tf_op jit(solution)/shard_map/ppermute | solution.py:15
  43.9 86.3 %while.15 = (s32[]{:T(128)}, f32[3,128,256]{2,0,1:T(4,128)S(1)}, s32[60,128]{1,0:T(8,128)}, bf16[3,416,256]{2,0,1:T(4,128)(2,1)S(1)}, bf16[3,3,61,128]{3,2,1,0:T...) while((s32[]{:T(128)}, f32[3,128,256]{2,0,1:T(4,128)S(1)}, ...), condition=%wide.region_1.2_spmd, body=%wide.region_0.1_spmd.sunk | while | flops 2856458 | bytes 3210441 | solution.py:57
  45.9 2.4 gather_fusion
  48.3 1.4 fusion.30
  51.6 2.4 gather_fusion
  57.4 2.4 gather_fusion
  63.1 2.4 gather_fusion
  65.6 1.4 fusion.30
  68.9 2.4 gather_fusion
  74.7 2.4 gather_fusion
  80.4 2.4 gather_fusion
  86.2 2.4 gather_fusion
  91.9 2.4 gather_fusion
  97.7 2.4 gather_fusion
  103.4 2.4 gather_fusion
  105.8 1.4 fusion.30
  109.2 2.4 gather_fusion
  114.9 2.4 gather_fusion
  120.7 2.4 gather_fusion
  126.4 2.4 gather_fusion
  131.8 456.1 %all-reduce.2.cloned.1.call-done = f32[2,128,128]{1,2,0:T(8,128)} async-done(((f32[2,128,128]{1,2,0:T(8,128)}), f32[2,128,128]{1,2,0:T(8,128)}) %all-reduce.2.cloned.1.call-update) | async-done | bytes 131088 | tf_op jit(solution)/shard_map/psum | solution.py:72
  (141 shorter events, 58.8 us)
Async XLA Ops:
  7.2 580.8 %all-reduce.2.cloned.1.call-start = ((), (), s32[]{:S(2)}) async-start(), calls=%async_computation | async-start | bytes 262144 | tf_op jit(solution)/shard_map/psum | solution.py:72
  11.3 11.6 %collective-permute-start.1 = (bf16[3,1,1,32,256]{4,0,3,2,1:T(4,128)(2,1)S(1)}, bf16[3,1,1,32,256]{4,0,3,2,1:T(4,128)(2,1)S(1)}, u32[]{:S(2)}, u32[]{:S(2)}) collective-permute-start(bf16[3,1,1,32,256]{4,0,3,2,1:T(4,128)(2,1)S(1)} %bitcast_select_fusion), channel_id=1, source_target_pairs={{16,0},{32,16},{48,32},{64,48},{80,64},{96,80},{112,96},{128,112},... | collective-permute-start | bytes 147464 | tf_op jit(solution)/shard_map/ppermute | solution.py:15
  20.1 3.2 collective-permute-start
  23.5 19.2 %collective-permute-start.3 = (bf16[3,3,1,32,256]{4,0,3,2,1:T(4,128)(2,1)S(1)}, bf16[3,3,1,32,256]{4,0,3,2,1:T(4,128)(2,1)S(1)}, u32[]{:S(2)}, u32[]{:S(2)}) collective-permute-start(bf16[3,3,1,32,256]{4,0,3,2,1:T(4,128)(2,1)S(1)} %pad_maximum_fusion.3), channel_id=1, source_target_pairs={{1,0},{2,1},{3,2},{4,3},{5,4},{6,5},{7,6},{8,7},{9,8},{10,9},{11,1... | collective-permute-start | bytes 442376 | tf_op jit(solution)/shard_map/ppermute | solution.py:15
  24.8 17.9 %collective-permute-start.2 = (bf16[3,3,1,32,256]{4,0,3,2,1:T(4,128)(2,1)S(1)}, bf16[3,3,1,32,256]{4,0,3,2,1:T(4,128)(2,1)S(1)}, u32[]{:S(2)}, u32[]{:S(2)}) collective-permute-start(bf16[3,3,1,32,256]{4,0,3,2,1:T(4,128)(2,1)S(1)} %pad_maximum_fusion.3), channel_id=1, source_target_pairs={{0,1},{1,2},{2,3},{3,4},{4,5},{5,6},{6,7},{7,8},{8,9},{9,10},{10,1... | collective-permute-start | bytes 442376 | tf_op jit(solution)/shard_map/ppermute | solution.py:14
  43.9 86.4 %copy-start = (bf16[3,128,128]{2,1,0:T(8,128)(2,1)S(1)}, bf16[3,128,128]{2,1,0:T(8,128)(2,1)}, u32[]{:S(2)}) copy-start(bf16[3,128,128]{2,1,0:T(8,128)(2,1)} %param.9) | copy-start | bytes 294916
  131.1 459.0 %copy-start.1 = (f32[2,128,128]{2,1,0:T(8,128)S(1)}, f32[2,128,128]{2,1,0:T(8,128)}, u32[]{:S(2)}) copy-start(f32[2,128,128]{2,1,0:T(8,128)} %param.15) | copy-start | bytes 393220
Sparse Core Ops, SparseCore 0:
  132.0 455.9 all-reduce.1
where the time goes:
time: 600 us; the launch traced here: 598 us
  waiting for transfers between devices  466 us (78%)
  local copies, waits for them, and re-layouts  56.9 us (9%)
  matrix products  24.1 us (4%)
  starting transfers between devices  19.9 us (3%)
  other arithmetic  16.2 us (3%)
  between operations  14.2 us (2%)
    psum x1, waiting for transfers between devices, local(): gram = lax.psum(partial_gram, ('wide', 'narrow')) / atoms_all  456 us
    gather x15, local copies, waits for them, and re-layouts, add_group(): jnp.take(extended, indices.reshape(-1), axis=1)  36 us
    dot_general x15, matrix products, add_group(): jnp.einsum('ijka,jkac->iac', blocks, picked, preferred_element_type=jnp.f...  21.1 us
    dynamic_slice x30, local copies, waits for them, and re-layouts, add_group(): blocks = lax.dynamic_slice_in_dim(hessian, 1 + group * 4, 4, 2)  15.7 us
  transfers between devices with their start and end apart: 5, of which 3 were waited for; matrix products, arithmetic and copies ran while one was open for 0% of the time, Pallas kernels for 0%

commit v1 on v0

v1 whole, which is shorter than its diff:
```python
import functools

import jax
import jax.numpy as jnp
from jax import lax
from jax.experimental import pallas as pl
from jax.experimental.pallas import tpu as pltpu
from jax.sharding import PartitionSpec as P

MESH = pl.DeviceIdType.MESH
F32 = jnp.float32
BF16 = jnp.bfloat16
A = 128
H = 32
V = 128
K = 60
ROWS = A + 9 * H
NISO = 16
CENTRE = ROWS // 2


def dot(x, y, dims=((1,), (0,))):
    return lax.dot_general(x, y, (dims, ((), ())), preferred_element_type=F32)


def split(x):
    high = x.astype(BF16)
    return high, (x - high.astype(F32)).astype(BF16)


def iota(shape, dim):
    return lax.broadcasted_iota(jnp.int32, shape, dim)


def combine_duplicates(nbr_ref, hess_ref, nbr_pad, h_pad, nbr_x, h_x):
    nbr_pad[0:64, :] = jnp.full((64, A), -1.0, F32)
    nbr_pad[64:64 + K, :] = nbr_ref[...].astype(F32)
    nbr_pad[64 + K:128, :] = jnp.full((64 - K, A), -2.0, F32)
    for cj in range(9):
        h_pad[cj, 0:64, :] = jnp.zeros((64, A), F32)
        h_pad[cj, 64:64 + K, :] = hess_ref[cj // 3, cj % 3, 1:1 + K, :].astype(F32)
        h_pad[cj, 64 + K:128, :] = jnp.zeros((64 - K, A), F32)

    def eight_slots(m, _):
        first = 64 + 8 * m
        here = nbr_pad[pl.ds(first, 8), :]
        sums = tuple(h_pad[cj, pl.ds(first, 8), :] for cj in range(9))

        def eight_shifts(g, sums):
            for t in range(8):
                back = first - (8 * g + t + 1)
                same = nbr_pad[pl.ds(back, 8), :] == here
                sums = tuple(
                    s + jnp.where(same, h_pad[cj, pl.ds(back, 8), :], 0.0) for cj, s in enumerate(sums)
                )
            return sums

        sums = lax.fori_loop(0, m + 1, eight_shifts, sums)
        for t in range(8):
            nbr_x[8 * m + t] = jnp.broadcast_to(here[t:t + 1, :] - CENTRE, (16, A)).astype(BF16)
            for cj in range(9):
                h_x[cj, 8 * m + t] = jnp.broadcast_to(sums[cj][t:t + 1, :], (16, A)).astype(BF16)
        return 0

    lax.fori_loop(0, 8, eight_slots, 0)


def weight_rows(block, nbr_x, h_x):
    ids = (iota((16, A), 0) + (block * 32 - CENTRE)).astype(F32)
    low, high = ids.astype(BF16), (ids + 16.0).astype(BF16)
    zero = jnp.zeros((16, A), BF16)

    def ten_slots(g, sums):
        for t in range(10):
            k = g * 10 + t
            row = nbr_x[k]
            at_low, at_high = row == low, row == high
            out = []
            for cj in range(9):
                value = h_x[cj, k]
                out.append(jnp.where(at_low, value, sums[2 * cj]))
                out.append(jnp.where(at_high, value, sums[2 * cj + 1]))
            sums = tuple(out)
        return sums

    return lax.fori_loop(0, K // 10, ten_slots, (zero,) * 18)


def kernel(
    n_wide, n_narrow, per_z, z_high,
    vec_ref, hess_ref, nbr_ref, halo_ref, lab_ref, mass_ref, rot_ref,
    gram_ref, out_ref,
    x_ref, nbr_pad, h_pad, nbr_x, h_x, w_local, w_halo, wt_halo, g_ref, first_ref, part_ref, second_ref, turned_ref,
    halo_send, halo_recv, send_sem, recv_sem,
):
    p, q = lax.axis_index("wide"), lax.axis_index("narrow")
    z_low = n_wide // per_z
    n_x = n_narrow // z_high
    plane, along = per_z * n_x, z_low * z_high
    in_plane = lax.div(q, z_high) * per_z + lax.rem(p, per_z)
    in_z = lax.rem(q, z_high) * z_low + lax.div(p, per_z)

    def plane_device(index):
        return (
            lax.div(p, per_z) * per_z + lax.rem(index, per_z),
            lax.div(index, per_z) * z_high + lax.rem(q, z_high),
        )

    def z_device(index):
        return (
            lax.rem(index, z_low) * per_z + lax.rem(p, per_z),
            lax.div(q, z_high) * z_high + lax.div(index, z_low),
        )

    has = {"up": p > 0, "down": p < n_wide - 1, "left": q > 0, "right": q < n_narrow - 1}
    where = {"up": (p - 1, q), "down": (p + 1, q), "left": (p, q - 1), "right": (p, q + 1)}

    for name, index in (("left", 0), ("right", 2)):
        @pl.when(jnp.logical_not(has[name]))
        def _():
            x_ref[1, index] = jnp.zeros((4, H, V), BF16)
    for name, index in (("up", 0), ("down", 2)):
        @pl.when(jnp.logical_not(has[name]))
        def _():
            x_ref[index] = jnp.zeros((3, 4, H, V), BF16)

    barrier = pltpu.get_barrier_semaphore()

    def greet(device):
        pl.semaphore_signal(barrier, inc=1, device_id=device, device_id_type=MESH)

    for name in has:
        @pl.when(has[name])
        def _():
            greet(where[name])

    def greet_plane(d, _):
        greet(plane_device(lax.rem(in_plane + d, plane)))
        return 0

    def greet_z(d, _):
        greet(z_device(lax.rem(in_z + d, along)))
        return 0

    lax.fori_loop(1, plane, greet_plane, 0)
    lax.fori_loop(1, along, greet_z, 0)

    masses = mass_ref[...]
    roots = lax.rsqrt(masses)
    roots = roots * (1.5 - 0.5 * masses * roots * roots)
    pick = lax.rem(iota((A, NISO), 0), NISO) == iota((A, NISO), 1)
    group = iota((A, V), 0)
    table = []
    for iso in range(2):
        column = jnp.sum(jnp.where(pick, roots[iso:iso + 1, :], 0.0), axis=1, keepdims=True)
        full = jnp.broadcast_to(column, (A, V))
        one = full.astype(BF16).astype(F32)
        two = (full - one).astype(BF16).astype(F32)
        three = full - one - two
        table.append(
            jnp.where(group < 16, one, jnp.where(group < 32, two, jnp.where(group < 48, three, 0.0))).astype(BF16)
        )
    table = jnp.concatenate(table, axis=1)
    classes = jnp.where(
        (lax.rem(group, NISO) == lab_ref[...]) & (group < 3 * NISO), 1.0, 0.0
    ).T.astype(BF16)
    factors = dot(classes, table)

    boundary = jnp.where(iota((A, H), 0) == halo_ref[...], 1.0, 0.0).astype(BF16)
    for j in range(3):
        x_ref[1, 1, j] = dot(boundary, vec_ref[j], ((0,), (0,))).astype(BF16)
    x_ref[1, 1, 3] = dot(boundary, classes, ((0,), (0,))).astype(BF16)

    greetings = plane + along - 2
    for name in has:
        greetings = greetings + has[name].astype(jnp.int32)
    pl.semaphore_wait(barrier, greetings)

    def halo_copy(j, at, name):
        number = at[0] * 3 + at[1]
        return pltpu.make_async_remote_copy(
            src_ref=x_ref.at[1, j], dst_ref=x_ref.at[at[0], at[1]],
            send_sem=halo_send.at[number], recv_sem=halo_recv.at[number],
            device_id=where[name], device_id_type=MESH,
        )

    to_right, to_left = halo_copy(1, (1, 0), "right"), halo_copy(1, (1, 2), "left")
    to_down = [halo_copy(j, (0, j), "down") for j in range(3)]
    to_up = [halo_copy(j, (2, j), "up") for j in range(3)]
    pl.when(has["right"])(to_right.start)
    pl.when(has["left"])(to_left.start)
    pl.when(has["down"])(to_down[1].start)
    pl.when(has["up"])(to_up[1].start)

    vectors = [vec_ref[j] for j in range(3)]
    stacked = vec_ref[...].reshape(3 * A, V)
    turned = stacked.astype(F32).T.astype(BF16)

    combine_duplicates(nbr_ref, hess_ref, nbr_pad, h_pad, nbr_x, h_x)

    def local_block(block, _):
        rows = weight_rows(block, nbr_x, h_x)
        for cj in range(9):
            at = pl.multiple_of(block * 32, 32)
            w_local[cj, pl.ds(at, 16), :] = rows[2 * cj]
            w_local[cj, pl.ds(pl.multiple_of(at + 16, 16), 16), :] = rows[2 * cj + 1]
        return 0

    lax.fori_loop(0, A // 32, local_block, 0)

    def halo_block(block, _):
        rows = weight_rows(block + A // 32, nbr_x, h_x)
        for cj in range(9):
            at = pl.multiple_of((cj % 3) * 9 * H + block * 32, 32)
            w_halo[cj // 3, pl.ds(at, 16), :] = rows[2 * cj]
            w_halo[cj // 3, pl.ds(pl.multiple_of(at + 16, 16), 16), :] = rows[2 * cj + 1]
        return 0

    lax.fori_loop(0, 5, halo_block, 0)

    pl.when(has["left"])(to_right.wait_recv)
    pl.when(has["down"])(to_down[0].start)
    pl.when(has["up"])(to_up[0].start)
    pl.when(has["right"])(to_left.wait_recv)
    pl.when(has["down"])(to_down[2].start)
    pl.when(has["up"])(to_up[2].start)

    lax.fori_loop(5, 9, halo_block, 0)

    own = iota((A, A), 0) == iota((A, A), 1)
    scaled = [
        (jnp.concatenate([v.astype(F32)] * 2, axis=1) * factors).astype(BF16) for v in vectors
    ]
    scaled = jnp.concatenate(scaled, axis=0)
    products = []
    for c in range(3):
        diagonal = jnp.concatenate(
            [jnp.where(own, hess_ref[c, j, 0:1, :].astype(F32), 0.0).astype(BF16) for j in range(3)], axis=1
        )
        near = jnp.concatenate([w_local[c * 3 + j].T for j in range(3)], axis=1)
        products.append(dot(diagonal, scaled) + dot(near, scaled))
        wt_halo[c * A:(c + 1) * A, :] = w_halo[c].T

    for name, copies in (("up", to_down), ("down", to_up)):
        @pl.when(has[name])
        def _():
            for copy in copies:
                copy.wait_recv()

    outer = x_ref[...].reshape(9, 4, H, V)
    far_factors = dot(outer[:, 3].reshape(9 * H, V), table)
    far = [
        (jnp.concatenate([outer[:, j].reshape(9 * H, V).astype(F32)] * 2, axis=1) * far_factors).astype(BF16)
        for j in range(3)
    ]
    product = jnp.concatenate(products, axis=0) + dot(wt_halo[...], jnp.concatenate(far, axis=0))
    image = product * jnp.concatenate([factors] * 3, axis=0)
    image_high, image_low = split(image)
    gram = dot(turned, image_high) + dot(turned, image_low)
    rows = 2 * V // plane
    for iso in range(2):
        g_ref[iso * (plane // 2):(iso + 1) * (plane // 2)] = gram[:, iso * V:(iso + 1) * V].reshape(plane // 2, rows, V)

    def scatter(d, _):
        target = lax.rem(in_plane + d, plane)
        pltpu.make_async_remote_copy(
            src_ref=g_ref.at[target], dst_ref=first_ref.at[plane - 1 - d],
            send_sem=send_sem.at[0], recv_sem=recv_sem.at[0],
            device_id=plane_device(target), device_id_type=MESH,
        ).start()
        return 0

    lax.fori_loop(1, plane, scatter, 0)

    def arrived(ref, number):
        pltpu.make_async_copy(ref, ref, recv_sem.at[number]).wait()

    def sent(ref, number):
        pltpu.make_async_copy(ref, ref, send_sem.at[number]).wait()

    rotations = [split(rot_ref[iso]) for iso in range(2)]
    for iso in range(2):
        high, low = image_high[:, iso * V:(iso + 1) * V], image_low[:, iso * V:(iso + 1) * V]
        r_high, r_low = rotations[iso]
        turned_ref[iso] = dot(high, r_high) + (dot(high, r_low) + dot(low, r_high))

    arrived(first_ref, 0)
    part_ref[0] = g_ref[in_plane] + jnp.sum(first_ref[...], axis=0)

    def exchange(d, _):
        target = lax.rem(in_z + d, along)
        pltpu.make_async_remote_copy(
            src_ref=part_ref.at[0], dst_ref=second_ref.at[along - 1 - d],
            send_sem=send_sem.at[1], recv_sem=recv_sem.at[1],
            device_id=z_device(target), device_id_type=MESH,
        ).start()
        return 0

    lax.fori_loop(1, along, exchange, 0)
    arrived(second_ref, 1)
    atoms_all = 3.0 * A * n_wide * n_narrow
    total = (part_ref[0] + jnp.sum(second_ref[...], axis=0)) / atoms_all
    sent(first_ref, 0)
    final_ref = part_ref.at[1]
    final_ref[...] = total

    def gather(d, _):
        target = lax.rem(in_plane + d, plane)
        pltpu.make_async_remote_copy(
            src_ref=final_ref, dst_ref=gram_ref.at[in_plane],
            send_sem=send_sem.at[2], recv_sem=recv_sem.at[2],
            device_id=plane_device(target), device_id_type=MESH,
        ).start()
        return 0

    lax.fori_loop(1, plane, gather, 0)
    gram_ref[in_plane] = total
    arrived(first_ref, 2)
    for iso in range(2):
        whole = gram_ref[iso * (plane // 2):(iso + 1) * (plane // 2)].reshape(V, V)
        high, low = split(whole)
        r_high, r_low = rotations[iso]
        m_high, m_low = split(dot(high, r_high) + (dot(high, r_low) + dot(low, r_high)))
        out_ref[iso] = (
            turned_ref[iso] - (dot(stacked, m_high) + dot(stacked, m_low))
        ).astype(BF16).reshape(3, A, V)

    sent(second_ref, 1)
    sent(first_ref, 2)
    pl.when(has["right"])(to_right.wait_send)
    pl.when(has["left"])(to_left.wait_send)
    for name, copies in (("down", to_down), ("up", to_up)):
        @pl.when(has[name])
        def _():
            for copy in copies:
                copy.wait_send()


def local(n_wide, n_narrow, per_z, z_high, vectors, hessian, neighbours, halo_atoms, labels, masses, rotation):
    plane = per_z * (n_narrow // z_high)
    along = (n_wide // per_z) * z_high
    rows = 2 * V // plane
    vmem = pl.BlockSpec(memory_space=pltpu.VMEM)
    gram, rotated = pl.pallas_call(
        functools.partial(kernel, n_wide, n_narrow, per_z, z_high),
        out_shape=(
            jax.ShapeDtypeStruct((plane, rows, V), F32),
            jax.ShapeDtypeStruct((2, 3, A, V), BF16),
        ),
        in_specs=[vmem] * 7,
        out_specs=(vmem, vmem),
        scratch_shapes=[
            pltpu.VMEM((3, 3, 4, H, V), BF16),
            pltpu.VMEM((128, A), F32),
            pltpu.VMEM((9, 128, A), F32),
            pltpu.VMEM((64, 16, A), BF16),
            pltpu.VMEM((9, 64, 16, A), BF16),
            pltpu.VMEM((9, A, A), BF16),
            pltpu.VMEM((3, 27 * H, A), BF16),
            pltpu.VMEM((3 * A, 27 * H), BF16),
            pltpu.VMEM((plane, rows, V), F32),
            pltpu.VMEM((plane - 1, rows, V), F32),
            pltpu.VMEM((2, rows, V), F32),
            pltpu.VMEM((along - 1, rows, V), F32),
            pltpu.VMEM((2, 3 * A, V), F32),
            pltpu.SemaphoreType.DMA((9,)),
            pltpu.SemaphoreType.DMA((9,)),
            pltpu.SemaphoreType.DMA((3,)),
            pltpu.SemaphoreType.DMA((3,)),
        ],
        compiler_params=pltpu.CompilerParams(
            collective_id=0, has_side_effects=True, vmem_limit_bytes=32 * 1024 * 1024
        ),
    )(vectors, hessian, neighbours, halo_atoms.reshape(1, H), labels.reshape(1, A), masses, rotation)
    return gram.reshape(2, V, V), rotated


def solution(mesh):
    n_wide, n_narrow = mesh.shape["wide"], mesh.shape["narrow"]
    per_z = n_wide // 4 if n_wide >= 16 else n_wide // 2
    z_high = 4 if n_narrow >= 16 else n_narrow // 2
    spread = ("wide", "narrow")
    return jax.shard_map(
        functools.partial(local, n_wide, n_narrow, per_z, z_high),
        mesh=mesh,
        in_specs=(
            P(None, spread, None),
            P(None, None, None, spread),
            P(None, spread),
            P(spread),
            P(spread),
            P(),
            P(),
        ),
        out_specs=(P(), P(None, None, spread, None)),
        check_vma=False,
    )
```

time: 600 us -> 52.3 us (0.09)
  waiting for transfers between devices: 466 us -> 0 us
  local copies, waits for them, and re-layouts: 56.9 us -> 5.47 us
  Pallas kernels: 0 us -> 45.9 us
  matrix products: 24.1 us -> 0 us
  starting transfers between devices: 19.9 us -> 0 us
  other arithmetic: 16.2 us -> 0 us
  between operations: 14.2 us -> 0.67 us
    psum x1 -> x0, waiting for transfers between devices: 456 us -> none  [local(): gram = lax.psum(partial_gram, ('wide', 'narrow')) / atoms_all]
    pallas_call x0 -> x1, Pallas kernels: none -> 45.9 us  [local(): pl.pallas_call(functools.partial(kernel, n_wide, n_narrow, per_z, z_high)...]
    gather x16 -> x0, local copies, waits for them, and re-layouts: 36.6 us -> none  [the longest x15 36 us: add_group(): jnp.take(extended, indices.reshape(-1), axis=1)]
    dot_general x23 -> x0, matrix products: 24.1 us -> none  [the longest x15 21.1 us: add_group(): jnp.einsum('ijka,jkac->iac', blocks, picked, preferred_element_type=jnp.f...]
    ppermute x4 -> x0, starting transfers between devices: 19.9 us -> none  [the longest x2 10.1 us: padded(): after = lax.ppermute(leading, axis, down)]
    dynamic_slice x30 -> x0, local copies, waits for them, and re-layouts: 15.7 us -> none  [add_group(): blocks = lax.dynamic_slice_in_dim(hessian, 1 + group * 4, 4, 2)]
    and x16 -> x0, other arithmetic: 11.2 us -> none  [the longest x15 10.6 us: add_group(): jnp.take(extended, indices.reshape(-1), axis=1)]
    ppermute x4 -> x0, waiting for transfers between devices: 10 us -> none  [the longest x2 9.65 us: padded(): after = lax.ppermute(leading, axis, down)]
  transfers between devices with their start and end apart: 5 -> 0, of which waited for: 3 -> 0; matrix products, arithmetic and copies ran while one was open for 0% -> 0% of each run, Pallas kernels for 0% -> 0%
where the time goes in v1:
time: 52.3 us; the launch traced here: 52 us
  Pallas kernels  45.9 us (88%)
  local copies, waits for them, and re-layouts  5.47 us (10%)
  between operations  0.67 us (1%)
    pallas_call x1, Pallas kernels, local(): pl.pallas_call(functools.partial(kernel, n_wide, n_narrow, per_z, z_high)...  45.9 us
    unnamed x16, local copies, waits for them, and re-layouts  5.47 us

profile of v1, /device:TPU:1, one launch (start us, length us, event | category | flops | bytes accessed | tf_op | source)
XLA Modules:
  0.0 52.0 jit_solution(14721075925198721528)
XLA Ops:
  0.6 0.0 copy-start.6
  0.6 0.0 copy-start.4
  0.7 0.0 copy-start.5
  0.7 0.6 %copy-done.6 = s32[128]{0:T(128)S(1)} copy-done((s32[128]{0:T(128)S(1)}, s32[128]{0:T(128)}, u32[]{:S(2)}) %copy-start.6) | copy-done | bytes 536
  1.3 0.0 copy-done.4
  1.3 0.0 copy-done.5
  1.3 0.0 copy-start
  1.3 0.9 %copy-done = bf16[3,3,61,128]{3,2,1,0:T(8,128)(2,1)S(1)} copy-done((bf16[3,3,61,128]{3,2,1,0:T(8,128)(2,1)S(1)}, bf16[3,3,61,128]{3,2,1,0:T(8,128)(2,1)}, u32[]{:S(2)}) %copy-start) | copy-done | bytes 140568
  2.2 0.0 copy-start.1
  2.2 0.9 %copy-done.1 = f32[2,128,128]{2,1,0:T(8,128)S(1)} copy-done((f32[2,128,128]{2,1,0:T(8,128)S(1)}, f32[2,128,128]{2,1,0:T(8,128)}, u32[]{:S(2)}) %copy-start.1) | copy-done | bytes 131096
  3.1 0.0 copy-start.2
  3.1 0.9 %copy-done.2 = bf16[3,128,128]{2,1,0:T(8,128)(2,1)S(1)} copy-done((bf16[3,128,128]{2,1,0:T(8,128)(2,1)S(1)}, bf16[3,128,128]{2,1,0:T(8,128)(2,1)}, u32[]{:S(2)}) %copy-start.2) | copy-done | bytes 98328
  4.0 0.0 copy-start.3
  4.0 0.8 %copy-done.3 = s32[60,128]{1,0:T(8,128)S(1)} copy-done((s32[60,128]{1,0:T(8,128)S(1)}, s32[60,128]{1,0:T(8,128)}, u32[]{:S(2)}) %copy-start.3) | copy-done | bytes 30744
  4.8 45.9 %shard_map.86 = (f32[32,8,128]{2,1,0:T(8,128)S(1)}, bf16[2,3,128,128]{3,2,1,0:T(8,128)(2,1)S(1)}) custom-call(bf16[3,128,128]{2,1,0:T(8,128)(2,1)S(1)} %copy-done.2, bf16[3,3,61,128]{3,2,1,0:T(8,128)(2,1)S(1)} %copy-done, s32[60,128]{1,0:T(8,128)S(1)} %copy-done.3, s32[1,32]{1,0:T(1,128)S(1)} %bitcast.4, s32[1,128]{1,0:T(1,128)S(1)} %bitcast.5, ...), custom_call_target="tpu_custom_call" | custom-call | tf_op jit(solution)/shard_map/pallas_call | solution.py:344
  50.7 0.7 %copy.11 = f32[2,128,128]{2,1,0:T(8,128)} copy(f32[2,128,128]{2,1,0:T(8,128)S(1)} %bitcast.3) | data formatting | bytes 262144
  51.4 0.7 %copy.12 = bf16[2,3,128,128]{3,2,1,0:T(8,128)(2,1)} copy(bf16[2,3,128,128]{3,2,1,0:T(8,128)(2,1)S(1)} %get-tuple-element.9) | data formatting | bytes 393216
Async XLA Ops:
  0.6 0.7 %copy-start.6 = (s32[128]{0:T(128)S(1)}, s32[128]{0:T(128)}, u32[]{:S(2)}) copy-start(s32[128]{0:T(128)} %param.11) | copy-start | bytes 1540
  0.6 0.7 %copy-start.4 = (f32[2,16]{1,0:T(2,128)S(1)}, f32[2,16]{1,0:T(2,128)}, u32[]{:S(2)}) copy-start(f32[2,16]{1,0:T(2,128)} %mass_ref.1) | copy-start | bytes 388
  0.7 0.7 %copy-start.5 = (s32[32]{0:T(128)S(1)}, s32[32]{0:T(128)}, u32[]{:S(2)}) copy-start(s32[32]{0:T(128)} %param.10) | copy-start | bytes 388
  1.3 0.9 %copy-start = (bf16[3,3,61,128]{3,2,1,0:T(8,128)(2,1)S(1)}, bf16[3,3,61,128]{3,2,1,0:T(8,128)(2,1)}, u32[]{:S(2)}) copy-start(bf16[3,3,61,128]{3,2,1,0:T(8,128)(2,1)} %hess_ref.1) | copy-start | bytes 421636
  2.2 0.9 %copy-start.1 = (f32[2,128,128]{2,1,0:T(8,128)S(1)}, f32[2,128,128]{2,1,0:T(8,128)}, u32[]{:S(2)}) copy-start(f32[2,128,128]{2,1,0:T(8,128)} %rot_ref.1) | copy-start | bytes 393220
  3.1 0.9 %copy-start.2 = (bf16[3,128,128]{2,1,0:T(8,128)(2,1)S(1)}, bf16[3,128,128]{2,1,0:T(8,128)(2,1)}, u32[]{:S(2)}) copy-start(bf16[3,128,128]{2,1,0:T(8,128)(2,1)} %vec_ref.1) | copy-start | bytes 294916
  4.0 0.8 %copy-start.3 = (s32[60,128]{1,0:T(8,128)S(1)}, s32[60,128]{1,0:T(8,128)}, u32[]{:S(2)}) copy-start(s32[60,128]{1,0:T(8,128)} %nbr_ref.1) | copy-start | bytes 92164

commit v2 on v1

--- a/solution.py
+++ b/solution.py
@@ -16,6 +16,8 @@
 K = 60
 ROWS = A + 9 * H
 NISO = 16
+CORNERS, EDGES = (0, 2, 6, 8), (1, 3, 4, 5, 7)
+PAY = 3 * H + H // 2
 CENTRE = ROWS // 2
 
 
@@ -88,10 +90,11 @@
 
 def kernel(
     n_wide, n_narrow, per_z, z_high,
+    vec_in, hess_in, nbr_in, halo_in, lab_in, mass_in, rot_in,
+    gram_ref, out_ref,
     vec_ref, hess_ref, nbr_ref, halo_ref, lab_ref, mass_ref, rot_ref,
-    gram_ref, out_ref,
     x_ref, nbr_pad, h_pad, nbr_x, h_x, w_local, w_halo, wt_halo, g_ref, first_ref, part_ref, second_ref, turned_ref,
-    halo_send, halo_recv, send_sem, recv_sem,
+    load_sem, halo_send, halo_recv, send_sem, recv_sem, relay_sem,
 ):
     p, q = lax.axis_index("wide"), lax.axis_index("narrow")
     z_low = n_wide // per_z
@@ -118,11 +121,11 @@
     for name, index in (("left", 0), ("right", 2)):
         @pl.when(jnp.logical_not(has[name]))
         def _():
-            x_ref[1, index] = jnp.zeros((4, H, V), BF16)
+            x_ref[1, index] = jnp.zeros((PAY, V), BF16)
     for name, index in (("up", 0), ("down", 2)):
         @pl.when(jnp.logical_not(has[name]))
         def _():
-            x_ref[index] = jnp.zeros((3, 4, H, V), BF16)
+            x_ref[index] = jnp.zeros((3, PAY, V), BF16)
 
     barrier = pltpu.get_barrier_semaphore()
 
@@ -142,8 +145,22 @@
         greet(z_device(lax.rem(in_z + d, along)))
         return 0
 
+    reach = along // 4
+    lax.fori_loop(1, reach + 1, greet_z, 0)
+    lax.fori_loop(along - reach, along, greet_z, 0)
     lax.fori_loop(1, plane, greet_plane, 0)
-    lax.fori_loop(1, along, greet_z, 0)
+
+    loads = [
+        pltpu.make_async_copy(source, target, load_sem.at[number])
+        for number, (source, target) in enumerate((
+            (halo_in, halo_ref), (lab_in, lab_ref), (mass_in, mass_ref), (vec_in, vec_ref),
+            (nbr_in, nbr_ref), (hess_in, hess_ref), (rot_in, rot_ref),
+        ))
+    ]
+    for load in loads:
+        load.start()
+    for load in loads[:4]:
+        load.wait()
 
     masses = mass_ref[...]
     roots = lax.rsqrt(masses)
@@ -161,17 +178,40 @@
             jnp.where(group < 16, one, jnp.where(group < 32, two, jnp.where(group < 48, three, 0.0))).astype(BF16)
         )
     table = jnp.concatenate(table, axis=1)
+    table_two = jnp.concatenate([jnp.zeros((V // 2, 2 * V), BF16), table[:V // 2]], axis=0)
+    half = lax.rem(group, V // 2)
     classes = jnp.where(
-        (lax.rem(group, NISO) == lab_ref[...]) & (group < 3 * NISO), 1.0, 0.0
+        (lax.rem(group, NISO) == lab_ref[...]) & (half < 3 * NISO), 1.0, 0.0
     ).T.astype(BF16)
     factors = dot(classes, table)
 
     boundary = jnp.where(iota((A, H), 0) == halo_ref[...], 1.0, 0.0).astype(BF16)
     for j in range(3):
-        x_ref[1, 1, j] = dot(boundary, vec_ref[j], ((0,), (0,))).astype(BF16)
-    x_ref[1, 1, 3] = dot(boundary, classes, ((0,), (0,))).astype(BF16)
-
-    greetings = plane + along - 2
+        x_ref[1, 1, j * H:(j + 1) * H, :] = dot(boundary, vec_ref[j], ((0,), (0,))).astype(BF16)
+    chosen = dot(boundary, classes, ((0,), (0,)))
+    x_ref[1, 1, 3 * H:, :] = jnp.where(
+        iota((H // 2, V), 1) < V // 2, chosen[:H // 2], chosen[H // 2:]
+    ).astype(BF16)
+
+    for load in loads[4:]:
+        load.wait()
+    vectors = [vec_ref[j] for j in range(3)]
+    stacked = vec_ref[...].reshape(3 * A, V)
+    turned = stacked.astype(F32).T.astype(BF16)
+
+    combine_duplicates(nbr_ref, hess_ref, nbr_pad, h_pad, nbr_x, h_x)
+
+    def local_block(block, _):
+        rows = weight_rows(block, nbr_x, h_x)
+        for cj in range(9):
+            at = pl.multiple_of(block * 32, 32)
+            w_local[cj, pl.ds(at, 16), :] = rows[2 * cj]
+            w_local[cj, pl.ds(pl.multiple_of(at + 16, 16), 16), :] = rows[2 * cj + 1]
+        return 0
+
+    lax.fori_loop(0, A // 32, local_block, 0)
+
+    greetings = plane - 1 + 2 * reach
     for name in has:
         greetings = greetings + has[name].astype(jnp.int32)
     pl.semaphore_wait(barrier, greetings)
@@ -192,31 +232,18 @@
     pl.when(has["down"])(to_down[1].start)
     pl.when(has["up"])(to_up[1].start)
 
-    vectors = [vec_ref[j] for j in range(3)]
-    stacked = vec_ref[...].reshape(3 * A, V)
-    turned = stacked.astype(F32).T.astype(BF16)
-
-    combine_duplicates(nbr_ref, hess_ref, nbr_pad, h_pad, nbr_x, h_x)
-
-    def local_block(block, _):
-        rows = weight_rows(block, nbr_x, h_x)
-        for cj in range(9):
-            at = pl.multiple_of(block * 32, 32)
-            w_local[cj, pl.ds(at, 16), :] = rows[2 * cj]
-            w_local[cj, pl.ds(pl.multiple_of(at + 16, 16), 16), :] = rows[2 * cj + 1]
-        return 0
-
-    lax.fori_loop(0, A // 32, local_block, 0)
+    for d in (reach, along - reach):
+        pl.semaphore_signal(relay_sem, inc=1, device_id=z_device(lax.rem(in_z + d, along)), device_id_type=MESH)
 
     def halo_block(block, _):
         rows = weight_rows(block + A // 32, nbr_x, h_x)
         for cj in range(9):
-            at = pl.multiple_of((cj % 3) * 9 * H + block * 32, 32)
-            w_halo[cj // 3, pl.ds(at, 16), :] = rows[2 * cj]
-            w_halo[cj // 3, pl.ds(pl.multiple_of(at + 16, 16), 16), :] = rows[2 * cj + 1]
+            at = (cj % 3) * H
+            w_halo[cj // 3, block, at:at + 16, :] = rows[2 * cj]
+            w_halo[cj // 3, block, at + 16:at + 32, :] = rows[2 * cj + 1]
         return 0
 
-    lax.fori_loop(0, 5, halo_block, 0)
+    lax.fori_loop(0, 8, halo_block, 0)
 
     pl.when(has["left"])(to_right.wait_recv)
     pl.when(has["down"])(to_down[0].start)
@@ -225,7 +252,7 @@
     pl.when(has["down"])(to_down[2].start)
     pl.when(has["up"])(to_up[2].start)
 
-    lax.fori_loop(5, 9, halo_block, 0)
+    lax.fori_loop(8, 9, halo_block, 0)
 
     own = iota((A, A), 0) == iota((A, A), 1)
     scaled = [
@@ -239,38 +266,59 @@
         )
         near = jnp.concatenate([w_local[c * 3 + j].T for j in range(3)], axis=1)
         products.append(dot(diagonal, scaled) + dot(near, scaled))
-        wt_halo[c * A:(c + 1) * A, :] = w_halo[c].T
+        wt_halo[c * A:(c + 1) * A, :] = jnp.concatenate([w_halo[c, b] for b in CORNERS], axis=0).T
+
+    def far_rows(blocks):
+        out = []
+        for b in blocks:
+            block = x_ref[b // 3, b % 3]
+            packed = block[3 * H:]
+            scale = jnp.concatenate([dot(packed, table), dot(packed, table_two)], axis=0)
+            for j in range(3):
+                rows = block[j * H:(j + 1) * H].astype(F32)
+                out.append((jnp.concatenate([rows, rows], axis=1) * scale).astype(BF16))
+        return jnp.concatenate(out, axis=0)
+
+    for name, copies in (("up", to_down), ("down", to_up)):
+        pl.when(has[name])(copies[1].wait_recv)
+    edge_rows = far_rows(EDGES)
+    for c in range(3):
+        edges = jnp.concatenate([w_halo[c, b] for b in EDGES], axis=0).T
+        products[c] += dot(edges, edge_rows)
+    early = jnp.concatenate(products, axis=0)
+    all_factors = jnp.concatenate([factors] * 3, axis=0)
 
     for name, copies in (("up", to_down), ("down", to_up)):
         @pl.when(has[name])
         def _():
-            for copy in copies:
-                copy.wait_recv()
-
-    outer = x_ref[...].reshape(9, 4, H, V)
-    far_factors = dot(outer[:, 3].reshape(9 * H, V), table)
-    far = [
-        (jnp.concatenate([outer[:, j].reshape(9 * H, V).astype(F32)] * 2, axis=1) * far_factors).astype(BF16)
-        for j in range(3)
-    ]
-    product = jnp.concatenate(products, axis=0) + dot(wt_halo[...], jnp.concatenate(far, axis=0))
-    image = product * jnp.concatenate([factors] * 3, axis=0)
+            copies[0].wait_recv()
+            copies[2].wait_recv()
+
+    product = early + dot(wt_halo[...], far_rows(CORNERS))
+    image = product * all_factors
     image_high, image_low = split(image)
     gram = dot(turned, image_high) + dot(turned, image_low)
     rows = 2 * V // plane
     for iso in range(2):
         g_ref[iso * (plane // 2):(iso + 1) * (plane // 2)] = gram[:, iso * V:(iso + 1) * V].reshape(plane // 2, rows, V)
 
-    def scatter(d, _):
+    def scatter(d):
         target = lax.rem(in_plane + d, plane)
         pltpu.make_async_remote_copy(
             src_ref=g_ref.at[target], dst_ref=first_ref.at[plane - 1 - d],
             send_sem=send_sem.at[0], recv_sem=recv_sem.at[0],
             device_id=plane_device(target), device_id_type=MESH,
         ).start()
-        return 0
-
-    lax.fori_loop(1, plane, scatter, 0)
+
+    def ring(distance, size):
+        return min(distance % size, -distance % size)
+
+    plane_order = sorted(
+        range(1, plane), key=lambda d: -ring(d // per_z, n_x) - ring(d // 2 % (per_z // 2), per_z // 2)
+    )
+    z_order = sorted(range(1, along), key=lambda d: -ring(d, along))
+    for d in plane_order:
+        scatter(d)
 
     def arrived(ref, number):
         pltpu.make_async_copy(ref, ref, recv_sem.at[number]).wait()
@@ -287,16 +335,17 @@
     arrived(first_ref, 0)
     part_ref[0] = g_ref[in_plane] + jnp.sum(first_ref[...], axis=0)
 
-    def exchange(d, _):
+    def exchange(d):
         target = lax.rem(in_z + d, along)
         pltpu.make_async_remote_copy(
             src_ref=part_ref.at[0], dst_ref=second_ref.at[along - 1 - d],
             send_sem=send_sem.at[1], recv_sem=recv_sem.at[1],
             device_id=z_device(target), device_id_type=MESH,
         ).start()
-        return 0
-
-    lax.fori_loop(1, along, exchange, 0)
+
+    pl.semaphore_wait(relay_sem, 2)
+    for d in z_order:
+        exchange(d)
     arrived(second_ref, 1)
     atoms_all = 3.0 * A * n_wide * n_narrow
     total = (part_ref[0] + jnp.sum(second_ref[...], axis=0)) / atoms_all
@@ -304,16 +353,16 @@
     final_ref = part_ref.at[1]
     final_ref[...] = total
 
-    def gather(d, _):
+    def gather(d):
         target = lax.rem(in_plane + d, plane)
         pltpu.make_async_remote_copy(
             src_ref=final_ref, dst_ref=gram_ref.at[in_plane],
             send_sem=send_sem.at[2], recv_sem=recv_sem.at[2],
             device_id=plane_device(target), device_id_type=MESH,
         ).start()
-        return 0
-
-    lax.fori_loop(1, plane, gather, 0)
+
+    for d in plane_order:
+        gather(d)
     gram_ref[in_plane] = total
     arrived(first_ref, 2)
     for iso in range(2):
@@ -344,32 +393,41 @@
     gram, rotated = pl.pallas_call(
         functools.partial(kernel, n_wide, n_narrow, per_z, z_high),
         out_shape=(
-            jax.ShapeDtypeStruct((plane, rows, V), F32),
-            jax.ShapeDtypeStruct((2, 3, A, V), BF16),
+            pltpu.VMEM((plane, rows, V), F32),
+            pltpu.VMEM((2, 3, A, V), BF16),
         ),
-        in_specs=[vmem] * 7,
+        in_specs=[pl.BlockSpec(memory_space=pltpu.HBM)] * 7,
         out_specs=(vmem, vmem),
         scratch_shapes=[
-            pltpu.VMEM((3, 3, 4, H, V), BF16),
+            pltpu.VMEM((3, A, V), BF16),
+            pltpu.VMEM((3, 3, 1 + K, A), BF16),
+            pltpu.VMEM((K, A), jnp.int32),
+            pltpu.VMEM((1, H), jnp.int32),
+            pltpu.VMEM((1, A), jnp.int32),
+            pltpu.VMEM((2, NISO), F32),
+            pltpu.VMEM((2, V, V), F32),
+            pltpu.VMEM((3, 3, PAY, V), BF16),
             pltpu.VMEM((128, A), F32),
             pltpu.VMEM((9, 128, A), F32),
             pltpu.VMEM((64, 16, A), BF16),
             pltpu.VMEM((9, 64, 16, A), BF16),
             pltpu.VMEM((9, A, A), BF16),
-            pltpu.VMEM((3, 27 * H, A), BF16),
-            pltpu.VMEM((3 * A, 27 * H), BF16),
+            pltpu.VMEM((3, 9, 3 * H, A), BF16),
+            pltpu.VMEM((3 * A, 12 * H), BF16),
             pltpu.VMEM((plane, rows, V), F32),
             pltpu.VMEM((plane - 1, rows, V), F32),
             pltpu.VMEM((2, rows, V), F32),
             pltpu.VMEM((along - 1, rows, V), F32),
             pltpu.VMEM((2, 3 * A, V), F32),
+            pltpu.SemaphoreType.DMA((7,)),
             pltpu.SemaphoreType.DMA((9,)),
             pltpu.SemaphoreType.DMA((9,)),
             pltpu.SemaphoreType.DMA((3,)),
             pltpu.SemaphoreType.DMA((3,)),
+            pltpu.SemaphoreType.REGULAR,
         ],
         compiler_params=pltpu.CompilerParams(
-            collective_id=0, has_side_effects=True, vmem_limit_bytes=32 * 1024 * 1024
+            collective_id=0, has_side_effects=True, vmem_limit_bytes=60 * 1024 * 1024
         ),
     )(vectors, hessian, neighbours, halo_atoms.reshape(1, H), labels.reshape(1, A), masses, rotation)
     return gram.reshape(2, V, V), rotated

time: 52.3 us -> 46.6 us (0.89)
  local copies, waits for them, and re-layouts: 5.47 us -> 1.33 us
  Pallas kernels: 45.9 us -> 44.5 us
    unnamed x16 -> x2, local copies, waits for them, and re-layouts: 5.47 us -> 1.33 us
    pallas_call x1, Pallas kernels: 45.9 us -> 44.5 us  [local(): pl.pallas_call(functools.partial(kernel, n_wide, n_narrow, per_z, z_high)...]
where the time goes in v2:
time: 46.6 us; the launch traced here: 46.4 us
  Pallas kernels  44.5 us (95%)
  local copies, waits for them, and re-layouts  1.33 us (3%)
  between operations  0.64 us (1%)
    pallas_call x1, Pallas kernels, local(): pl.pallas_call(functools.partial(kernel, n_wide, n_narrow, per_z, z_high)...  44.5 us
    unnamed x2, local copies, waits for them, and re-layouts  1.33 us

profile of v2, /device:TPU:1, one launch (start us, length us, event | category | flops | bytes accessed | tf_op | source)
XLA Modules:
  0.0 46.4 jit_solution(16562166350913838500)
XLA Ops:
  0.6 44.5 %shard_map.86 = (f32[32,8,128]{2,1,0:T(8,128)S(1)}, bf16[2,3,128,128]{3,2,1,0:T(8,128)(2,1)S(1)}) custom-call(bf16[3,128,128]{2,1,0:T(8,128)(2,1)} %vec_in.1, bf16[3,3,61,128]{3,2,1,0:T(8,128)(2,1)} %hess_in.1, s32[60,128]{1,0:T(8,128)} %nbr_in.1, s32[1,32]{1,0:T(1,128)} %bitcast.4, s32[1,128]{1,0:T(1,128)} %bitcast.5, f32[2,16]{1,0:T(2,128)} %mass_in.1, ...), custom_call_target="tpu_custom_call" | custom-call | tf_op jit(solution)/shard_map/pallas_call | solution.py:393
  45.1 0.7 %copy.11 = f32[2,128,128]{2,1,0:T(8,128)} copy(f32[2,128,128]{2,1,0:T(8,128)S(1)} %bitcast.3) | data formatting | bytes 262144
  45.8 0.7 %copy.12 = bf16[2,3,128,128]{3,2,1,0:T(8,128)(2,1)} copy(bf16[2,3,128,128]{3,2,1,0:T(8,128)(2,1)S(1)} %get-tuple-element.7) | data formatting | bytes 393216

commit v3 on v2

--- a/solution.py
+++ b/solution.py
@@ -14,6 +14,7 @@
 H = 32
 V = 128
 K = 60
+UNROLL = 30
 ROWS = A + 9 * H
 NISO = 16
 CORNERS, EDGES = (0, 2, 6, 8), (1, 3, 4, 5, 7)
@@ -72,9 +73,9 @@
     low, high = ids.astype(BF16), (ids + 16.0).astype(BF16)
     zero = jnp.zeros((16, A), BF16)
 
-    def ten_slots(g, sums):
-        for t in range(10):
-            k = g * 10 + t
+    def many_slots(g, sums):
+        for t in range(UNROLL):
+            k = g * UNROLL + t
             row = nbr_x[k]
             at_low, at_high = row == low, row == high
             out = []
@@ -85,7 +86,7 @@
             sums = tuple(out)
         return sums
 
-    return lax.fori_loop(0, K // 10, ten_slots, (zero,) * 18)
+    return lax.fori_loop(0, K // UNROLL, many_slots, (zero,) * 18)
 
 
 def kernel(
@@ -103,17 +104,27 @@
     in_plane = lax.div(q, z_high) * per_z + lax.rem(p, per_z)
     in_z = lax.rem(q, z_high) * z_low + lax.div(p, per_z)
 
-    def plane_device(index):
-        return (
-            lax.div(p, per_z) * per_z + lax.rem(index, per_z),
-            lax.div(index, per_z) * z_high + lax.rem(q, z_high),
-        )
-
-    def z_device(index):
-        return (
-            lax.rem(index, z_low) * per_z + lax.rem(p, per_z),
-            lax.div(q, z_high) * z_high + lax.div(index, z_low),
-        )
+    n_y = per_z // 2
+    x_at, y_at, core = lax.div(q, z_high), lax.div(lax.rem(p, per_z), 2), lax.rem(p, 2)
+    p_plane, q_plane = p - lax.rem(p, per_z), lax.rem(q, z_high)
+    p_z, q_z = lax.rem(p, per_z), q - lax.rem(q, z_high)
+    xs = [lax.rem(x_at + d, n_x) for d in range(n_x)]
+    ys = [lax.rem(y_at + d, n_y) * 2 for d in range(n_y)]
+    cores = [core, 1 - core]
+    tops = [q_plane + x * z_high for x in xs]
+    lows = [[y + c for c in cores] for y in ys]
+
+    def plane_device(d):
+        dx, dy, dc = d // per_z, d // 2 % n_y, d % 2
+        return (p_plane + lows[dy][dc], tops[dx]), xs[dx] * per_z + lows[dy][dc]
+
+    def z_device(d):
+        at = lax.rem(in_z + d, along)
+        return lax.rem(at, z_low) * per_z + p_z, q_z + lax.div(at, z_low)
+
+    def back(d):
+        dx, dy, dc = d // per_z, d // 2 % n_y, d % 2
+        return (-dx % n_x) * per_z + (-dy % n_y) * 2 + dc
 
     has = {"up": p > 0, "down": p < n_wide - 1, "left": q > 0, "right": q < n_narrow - 1}
     where = {"up": (p - 1, q), "down": (p + 1, q), "left": (p, q - 1), "right": (p, q + 1)}
@@ -137,18 +148,12 @@
         def _():
             greet(where[name])
 
-    def greet_plane(d, _):
-        greet(plane_device(lax.rem(in_plane + d, plane)))
-        return 0
-
-    def greet_z(d, _):
-        greet(z_device(lax.rem(in_z + d, along)))
-        return 0
-
     reach = along // 4
-    lax.fori_loop(1, reach + 1, greet_z, 0)
-    lax.fori_loop(along - reach, along, greet_z, 0)
-    lax.fori_loop(1, plane, greet_plane, 0)
+    for d in range(reach, 0, -1):
+        greet(z_device(d))
+        greet(z_device(along - d))
+    for d in range(1, plane):
+        greet(plane_device(d)[0])
 
     loads = [
         pltpu.make_async_copy(source, target, load_sem.at[number])
@@ -209,7 +214,7 @@
             w_local[cj, pl.ds(pl.multiple_of(at + 16, 16), 16), :] = rows[2 * cj + 1]
         return 0
 
-    lax.fori_loop(0, A // 32, local_block, 0)
+    lax.fori_loop(0, 2, local_block, 0)
 
     greetings = plane - 1 + 2 * reach
     for name in has:
@@ -233,7 +238,7 @@
     pl.when(has["up"])(to_up[1].start)
 
     for d in (reach, along - reach):
-        pl.semaphore_signal(relay_sem, inc=1, device_id=z_device(lax.rem(in_z + d, along)), device_id_type=MESH)
+        pl.semaphore_signal(relay_sem, inc=1, device_id=z_device(d), device_id_type=MESH)
 
     def halo_block(block, _):
         rows = weight_rows(block + A // 32, nbr_x, h_x)
@@ -243,16 +248,8 @@
             w_halo[cj // 3, block, at + 16:at + 32, :] = rows[2 * cj + 1]
         return 0
 
-    lax.fori_loop(0, 8, halo_block, 0)
-
-    pl.when(has["left"])(to_right.wait_recv)
-    pl.when(has["down"])(to_down[0].start)
-    pl.when(has["up"])(to_up[0].start)
-    pl.when(has["right"])(to_left.wait_recv)
-    pl.when(has["down"])(to_down[2].start)
-    pl.when(has["up"])(to_up[2].start)
-
-    lax.fori_loop(8, 9, halo_block, 0)
+    lax.fori_loop(2, A // 32, local_block, 0)
+    lax.fori_loop(0, 9, halo_block, 0)
 
     own = iota((A, A), 0) == iota((A, A), 1)
     scaled = [
@@ -279,6 +276,13 @@
                 out.append((jnp.concatenate([rows, rows], axis=1) * scale).astype(BF16))
         return jnp.concatenate(out, axis=0)
 
+    pl.when(has["left"])(to_right.wait_recv)
+    pl.when(has["down"])(to_down[0].start)
+    pl.when(has["up"])(to_up[0].start)
+    pl.when(has["right"])(to_left.wait_recv)
+    pl.when(has["down"])(to_down[2].start)
+    pl.when(has["up"])(to_up[2].start)
+
     for name, copies in (("up", to_down), ("down", to_up)):
         pl.when(has[name])(copies[1].wait_recv)
     edge_rows = far_rows(EDGES)
@@ -303,18 +307,18 @@
         g_ref[iso * (plane // 2):(iso + 1) * (plane // 2)] = gram[:, iso * V:(iso + 1) * V].reshape(plane // 2, rows, V)
 
     def scatter(d):
-        target = lax.rem(in_plane + d, plane)
+        device, target = plane_device(d)
         pltpu.make_async_remote_copy(
-            src_ref=g_ref.at[target], dst_ref=first_ref.at[plane - 1 - d],
+            src_ref=g_ref.at[target], dst_ref=first_ref.at[back(d) - 1],
             send_sem=send_sem.at[0], recv_sem=recv_sem.at[0],
-            device_id=plane_device(target), device_id_type=MESH,
+            device_id=device, device_id_type=MESH,
         ).start()
 
     def ring(distance, size):
         return min(distance % size, -distance % size)
 
     plane_order = sorted(
-        range(1, plane), key=lambda d: -ring(d // per_z, n_x) - ring(d // 2 % (per_z // 2), per_z // 2)
+        range(1, plane), key=lambda d: -ring(d // per_z, n_x) - ring(d // 2 % n_y, n_y)
     )
     z_order = sorted(range(1, along), key=lambda d: -ring(d, along))
     for d in plane_order:
@@ -336,11 +340,10 @@
     part_ref[0] = g_ref[in_plane] + jnp.sum(first_ref[...], axis=0)
 
     def exchange(d):
-        target = lax.rem(in_z + d, along)
         pltpu.make_async_remote_copy(
             src_ref=part_ref.at[0], dst_ref=second_ref.at[along - 1 - d],
             send_sem=send_sem.at[1], recv_sem=recv_sem.at[1],
-            device_id=z_device(target), device_id_type=MESH,
+            device_id=z_device(d), device_id_type=MESH,
         ).start()
 
     pl.semaphore_wait(relay_sem, 2)
@@ -354,11 +357,11 @@
     final_ref[...] = total
 
     def gather(d):
-        target = lax.rem(in_plane + d, plane)
+        device, _ = plane_device(d)
         pltpu.make_async_remote_copy(
             src_ref=final_ref, dst_ref=gram_ref.at[in_plane],
             send_sem=send_sem.at[2], recv_sem=recv_sem.at[2],
-            device_id=plane_device(target), device_id_type=MESH,
+            device_id=device, device_id_type=MESH,
         ).start()
 
     for d in plane_order:

time: 46.6 us -> 44.8 us (0.961)
  Pallas kernels: 44.5 us -> 42.7 us
    pallas_call x1, Pallas kernels: 44.5 us -> 42.7 us  [local(): pl.pallas_call(functools.partial(kernel, n_wide, n_narrow, per_z, z_high)...]
where the time goes in v3:
time: 44.8 us; the launch traced here: 44.7 us
  Pallas kernels  42.7 us (95%)
  local copies, waits for them, and re-layouts  1.33 us (3%)
  between operations  0.64 us (1%)
    pallas_call x1, Pallas kernels, local(): pl.pallas_call(functools.partial(kernel, n_wide, n_narrow, per_z, z_high)...  42.7 us
    unnamed x2, local copies, waits for them, and re-layouts  1.33 us

profile of v3, /device:TPU:1, one launch (start us, length us, event | category | flops | bytes accessed | tf_op | source)
XLA Modules:
  0.0 44.7 jit_solution(5316594394224716442)
XLA Ops:
  0.6 42.7 %shard_map.86 = (f32[32,8,128]{2,1,0:T(8,128)S(1)}, bf16[2,3,128,128]{3,2,1,0:T(8,128)(2,1)S(1)}) custom-call(bf16[3,128,128]{2,1,0:T(8,128)(2,1)} %vec_in.1, bf16[3,3,61,128]{3,2,1,0:T(8,128)(2,1)} %hess_in.1, s32[60,128]{1,0:T(8,128)} %nbr_in.1, s32[1,32]{1,0:T(1,128)} %bitcast.4, s32[1,128]{1,0:T(1,128)} %bitcast.5, f32[2,16]{1,0:T(2,128)} %mass_in.1, ...), custom_call_target="tpu_custom_call" | custom-call | tf_op jit(solution)/shard_map/pallas_call | solution.py:396
  43.3 0.7 %copy.11 = f32[2,128,128]{2,1,0:T(8,128)} copy(f32[2,128,128]{2,1,0:T(8,128)S(1)} %bitcast.3) | data formatting | bytes 262144
  44.0 0.7 %copy.12 = bf16[2,3,128,128]{3,2,1,0:T(8,128)(2,1)} copy(bf16[2,3,128,128]{3,2,1,0:T(8,128)(2,1)S(1)} %get-tuple-element.7) | data formatting | bytes 393216

commit v4 on v3

--- a/solution.py
+++ b/solution.py
@@ -92,9 +92,9 @@
 def kernel(
     n_wide, n_narrow, per_z, z_high,
     vec_in, hess_in, nbr_in, halo_in, lab_in, mass_in, rot_in,
-    gram_ref, out_ref,
+    gram_ref, turned_ref,
     vec_ref, hess_ref, nbr_ref, halo_ref, lab_ref, mass_ref, rot_ref,
-    x_ref, nbr_pad, h_pad, nbr_x, h_x, w_local, w_halo, wt_halo, g_ref, first_ref, part_ref, second_ref, turned_ref,
+    x_ref, nbr_pad, h_pad, nbr_x, h_x, w_local, w_halo, wt_halo, g_ref, first_ref, part_ref, second_ref,
     load_sem, halo_send, halo_recv, send_sem, recv_sem, relay_sem,
 ):
     p, q = lax.axis_index("wide"), lax.axis_index("narrow")
@@ -251,6 +251,13 @@
     lax.fori_loop(2, A // 32, local_block, 0)
     lax.fori_loop(0, 9, halo_block, 0)
 
+    pl.when(has["left"])(to_right.wait_recv)
+    pl.when(has["down"])(to_down[0].start)
+    pl.when(has["up"])(to_up[0].start)
+    pl.when(has["right"])(to_left.wait_recv)
+    pl.when(has["down"])(to_down[2].start)
+    pl.when(has["up"])(to_up[2].start)
+
     own = iota((A, A), 0) == iota((A, A), 1)
     scaled = [
         (jnp.concatenate([v.astype(F32)] * 2, axis=1) * factors).astype(BF16) for v in vectors
@@ -276,13 +283,6 @@
                 out.append((jnp.concatenate([rows, rows], axis=1) * scale).astype(BF16))
         return jnp.concatenate(out, axis=0)
 
-    pl.when(has["left"])(to_right.wait_recv)
-    pl.when(has["down"])(to_down[0].start)
-    pl.when(has["up"])(to_up[0].start)
-    pl.when(has["right"])(to_left.wait_recv)
-    pl.when(has["down"])(to_down[2].start)
-    pl.when(has["up"])(to_up[2].start)
-
     for name, copies in (("up", to_down), ("down", to_up)):
         pl.when(has[name])(copies[1].wait_recv)
     edge_rows = far_rows(EDGES)
@@ -291,6 +291,14 @@
         products[c] += dot(edges, edge_rows)
     early = jnp.concatenate(products, axis=0)
     all_factors = jnp.concatenate([factors] * 3, axis=0)
+    first_high, first_low = split(early * all_factors)
+    first_gram = dot(turned, first_high) + dot(turned, first_low)
+    corner_weights = wt_halo[...]
+    corner_left = []
+    for iso in range(2):
+        scale = jnp.concatenate([all_factors[:, iso * V:(iso + 1) * V]] * 3, axis=1)
+        high, low = split(corner_weights.astype(F32) * scale)
+        corner_left.append(split(dot(turned, high) + dot(turned, low)))
 
     for name, copies in (("up", to_down), ("down", to_up)):
         @pl.when(has[name])
@@ -298,13 +306,13 @@
             copies[0].wait_recv()
             copies[2].wait_recv()
 
-    product = early + dot(wt_halo[...], far_rows(CORNERS))
-    image = product * all_factors
-    image_high, image_low = split(image)
-    gram = dot(turned, image_high) + dot(turned, image_low)
+    corner_rows = far_rows(CORNERS)
     rows = 2 * V // plane
     for iso in range(2):
-        g_ref[iso * (plane // 2):(iso + 1) * (plane // 2)] = gram[:, iso * V:(iso + 1) * V].reshape(plane // 2, rows, V)
+        high, low = corner_left[iso]
+        right = corner_rows[:, iso * V:(iso + 1) * V]
+        gram = first_gram[:, iso * V:(iso + 1) * V] + (dot(high, right) + dot(low, right))
+        g_ref[iso * (plane // 2):(iso + 1) * (plane // 2)] = gram.reshape(plane // 2, rows, V)
 
     def scatter(d):
         device, target = plane_device(d)
@@ -330,6 +338,8 @@
     def sent(ref, number):
         pltpu.make_async_copy(ref, ref, send_sem.at[number]).wait()
 
+    product = early + dot(corner_weights, corner_rows)
+    image_high, image_low = split(product * all_factors)
     rotations = [split(rot_ref[iso]) for iso in range(2)]
     for iso in range(2):
         high, low = image_high[:, iso * V:(iso + 1) * V], image_low[:, iso * V:(iso + 1) * V]
@@ -368,15 +378,6 @@
         gather(d)
     gram_ref[in_plane] = total
     arrived(first_ref, 2)
-    for iso in range(2):
-        whole = gram_ref[iso * (plane // 2):(iso + 1) * (plane // 2)].reshape(V, V)
-        high, low = split(whole)
-        r_high, r_low = rotations[iso]
-        m_high, m_low = split(dot(high, r_high) + (dot(high, r_low) + dot(low, r_high)))
-        out_ref[iso] = (
-            turned_ref[iso] - (dot(stacked, m_high) + dot(stacked, m_low))
-        ).astype(BF16).reshape(3, A, V)
-
     sent(second_ref, 1)
     sent(first_ref, 2)
     pl.when(has["right"])(to_right.wait_send)
@@ -388,16 +389,41 @@
                 copy.wait_send()
 
 
+def finish(gram_ref, turned_ref, vec_in, rot_in, gram_out, out_ref, vec_ref, rot_ref, rotated_ref, sem):
+    loads = [
+        pltpu.make_async_copy(vec_in, vec_ref, sem.at[0]),
+        pltpu.make_async_copy(rot_in, rot_ref, sem.at[1]),
+    ]
+    stores = [pltpu.make_async_copy(gram_ref, gram_out, sem.at[2])]
+    for copy in loads + stores:
+        copy.start()
+    for load in loads:
+        load.wait()
+    half = gram_ref.shape[0] // 2
+    stacked = vec_ref[...].reshape(3 * A, V)
+    for iso in range(2):
+        high, low = split(gram_ref[iso * half:(iso + 1) * half].reshape(V, V))
+        r_high, r_low = split(rot_ref[iso])
+        m_high, m_low = split(dot(high, r_high) + (dot(high, r_low) + dot(low, r_high)))
+        rotated_ref[iso] = (
+            turned_ref[iso] - (dot(stacked, m_high) + dot(stacked, m_low))
+        ).astype(BF16).reshape(3, A, V)
+        stores.append(pltpu.make_async_copy(rotated_ref.at[iso], out_ref.at[iso], sem.at[3 + iso]))
+        stores[-1].start()
+    for store in stores:
+        store.wait()
+
+
 def local(n_wide, n_narrow, per_z, z_high, vectors, hessian, neighbours, halo_atoms, labels, masses, rotation):
     plane = per_z * (n_narrow // z_high)
     along = (n_wide // per_z) * z_high
     rows = 2 * V // plane
     vmem = pl.BlockSpec(memory_space=pltpu.VMEM)
-    gram, rotated = pl.pallas_call(
+    gram, turned = pl.pallas_call(
         functools.partial(kernel, n_wide, n_narrow, per_z, z_high),
         out_shape=(
             pltpu.VMEM((plane, rows, V), F32),
-            pltpu.VMEM((2, 3, A, V), BF16),
+            pltpu.VMEM((2, 3 * A, V), F32),
         ),
         in_specs=[pl.BlockSpec(memory_space=pltpu.HBM)] * 7,
         out_specs=(vmem, vmem),
@@ -421,7 +447,6 @@
             pltpu.VMEM((plane - 1, rows, V), F32),
             pltpu.VMEM((2, rows, V), F32),
             pltpu.VMEM((along - 1, rows, V), F32),
-            pltpu.VMEM((2, 3 * A, V), F32),
             pltpu.SemaphoreType.DMA((7,)),
             pltpu.SemaphoreType.DMA((9,)),
             pltpu.SemaphoreType.DMA((9,)),
@@ -433,6 +458,23 @@
             collective_id=0, has_side_effects=True, vmem_limit_bytes=60 * 1024 * 1024
         ),
     )(vectors, hessian, neighbours, halo_atoms.reshape(1, H), labels.reshape(1, A), masses, rotation)
+    anywhere = pl.BlockSpec(memory_space=pl.ANY)
+    gram, rotated = pl.pallas_call(
+        finish,
+        out_shape=(
+            jax.ShapeDtypeStruct((plane, rows, V), F32),
+            jax.ShapeDtypeStruct((2, 3, A, V), BF16),
+        ),
+        in_specs=[vmem, vmem, anywhere, anywhere],
+        out_specs=(anywhere, anywhere),
+        scratch_shapes=[
+            pltpu.VMEM((3, A, V), BF16),
+            pltpu.VMEM((2, V, V), F32),
+            pltpu.VMEM((2, 3, A, V), BF16),
+            pltpu.SemaphoreType.DMA((5,)),
+        ],
+        compiler_params=pltpu.CompilerParams(vmem_limit_bytes=8 * 1024 * 1024),
+    )(gram, turned, vectors, rotation)
     return gram.reshape(2, V, V), rotated
 
 

time: 44.8 us -> 44.2 us (0.987)
  local copies, waits for them, and re-layouts: 1.33 us -> 0.01 us
  Pallas kernels: 42.7 us -> 43.4 us
    pallas_call x0 -> x1, Pallas kernels: none -> 1.45 us  [local(): pl.pallas_call(finish, out_shape=(jax.ShapeDtypeStruct((plane, rows, V),...]
    unnamed x2 -> x4, local copies, waits for them, and re-layouts: 1.33 us -> 0.01 us
    pallas_call x1, Pallas kernels: 42.7 us -> 41.9 us  [local(): pl.pallas_call(functools.partial(kernel, n_wide, n_narrow, per_z, z_high)...]
where the time goes in v4:
time: 44.2 us; the launch traced here: 44.1 us
  Pallas kernels  43.4 us (98%)
  between operations  0.67 us (2%)
    pallas_call x1, Pallas kernels, local(): pl.pallas_call(functools.partial(kernel, n_wide, n_narrow, per_z, z_high)...  41.9 us
    pallas_call x1, Pallas kernels, local(): pl.pallas_call(finish, out_shape=(jax.ShapeDtypeStruct((plane, rows, V),...  1.45 us

profile of v4, /device:TPU:1, one launch (start us, length us, event | category | flops | bytes accessed | tf_op | source)
XLA Modules:
  0.0 44.1 jit_solution(15763170500762508944)
XLA Ops:
  0.6 0.0 copy-start
  0.6 0.0 copy-start.1
  0.7 41.9 %shard_map.86 = (f32[32,8,128]{2,1,0:T(8,128)S(1)}, f32[2,384,128]{2,1,0:T(8,128)S(1)}) custom-call(bf16[3,128,128]{2,1,0:T(8,128)(2,1)} %vec_in.3, bf16[3,3,61,128]{3,2,1,0:T(8,128)(2,1)} %hess_in.1, s32[60,128]{1,0:T(8,128)} %nbr_in.1, s32[1,32]{1,0:T(1,128)} %bitcast.3, s32[1,128]{1,0:T(1,128)} %bitcast.4, f32[2,16]{1,0:T(2,128)} %mass_in.1, ...), custom_call_target="tpu_custom_call" | custom-call | tf_op jit(solution)/shard_map/pallas_call | solution.py:422
  42.6 0.0 copy-done
  42.6 0.0 copy-done.1
  42.6 1.4 %shard_map.87 = (f32[32,8,128]{2,1,0:T(8,128)}, bf16[2,3,128,128]{3,2,1,0:T(8,128)(2,1)}) custom-call(f32[32,8,128]{2,1,0:T(8,128)S(1)} %get-tuple-element.6.gram_ref, f32[2,384,128]{2,1,0:T(8,128)S(1)} %get-tuple-element.7.turned_ref, bf16[3,128,128]{2,1,0:T(8,128)(2,1)S(1)} %copy-done.1, f32[2,128,128]{2,1,0:T(8,128)S(1)} %copy-done), custom_call_target="tpu_custom_call" | custom-call | tf_op jit(solution)/shard_map/pallas_call | solution.py:462
Async XLA Ops:
  0.6 42.0 %copy-start = (f32[2,128,128]{2,1,0:T(8,128)S(1)}, f32[2,128,128]{2,1,0:T(8,128)}, u32[]{:S(2)}) copy-start(f32[2,128,128]{2,1,0:T(8,128)} %rot_in.3) | copy-start | bytes 393220
  0.6 42.0 %copy-start.1 = (bf16[3,128,128]{2,1,0:T(8,128)(2,1)S(1)}, bf16[3,128,128]{2,1,0:T(8,128)(2,1)}, u32[]{:S(2)}) copy-start(bf16[3,128,128]{2,1,0:T(8,128)(2,1)} %vec_in.3) | copy-start | bytes 294916

commit v5 on v4

--- a/solution.py
+++ b/solution.py
@@ -389,26 +389,19 @@
                 copy.wait_send()
 
 
-def finish(gram_ref, turned_ref, vec_in, rot_in, gram_out, out_ref, vec_ref, rot_ref, rotated_ref, sem):
-    loads = [
-        pltpu.make_async_copy(vec_in, vec_ref, sem.at[0]),
-        pltpu.make_async_copy(rot_in, rot_ref, sem.at[1]),
-    ]
+def finish(gram_ref, turned_ref, vec_ref, rot_ref, gram_out, out_ref, rotated_ref, sem):
     stores = [pltpu.make_async_copy(gram_ref, gram_out, sem.at[2])]
-    for copy in loads + stores:
-        copy.start()
-    for load in loads:
-        load.wait()
+    stores[0].start()
     half = gram_ref.shape[0] // 2
-    stacked = vec_ref[...].reshape(3 * A, V)
     for iso in range(2):
         high, low = split(gram_ref[iso * half:(iso + 1) * half].reshape(V, V))
         r_high, r_low = split(rot_ref[iso])
         m_high, m_low = split(dot(high, r_high) + (dot(high, r_low) + dot(low, r_high)))
+        vectors = vec_ref[...].reshape(3 * A, V)
         rotated_ref[iso] = (
-            turned_ref[iso] - (dot(stacked, m_high) + dot(stacked, m_low))
+            turned_ref[iso] - (dot(vectors, m_high) + dot(vectors, m_low))
         ).astype(BF16).reshape(3, A, V)
-        stores.append(pltpu.make_async_copy(rotated_ref.at[iso], out_ref.at[iso], sem.at[3 + iso]))
+        stores.append(pltpu.make_async_copy(rotated_ref.at[iso], out_ref.at[iso], sem.at[iso]))
         stores[-1].start()
     for store in stores:
         store.wait()
@@ -465,13 +458,11 @@
             jax.ShapeDtypeStruct((plane, rows, V), F32),
             jax.ShapeDtypeStruct((2, 3, A, V), BF16),
         ),
-        in_specs=[vmem, vmem, anywhere, anywhere],
+        in_specs=[vmem] * 4,
         out_specs=(anywhere, anywhere),
         scratch_shapes=[
-            pltpu.VMEM((3, A, V), BF16),
-            pltpu.VMEM((2, V, V), F32),
             pltpu.VMEM((2, 3, A, V), BF16),
-            pltpu.SemaphoreType.DMA((5,)),
+            pltpu.SemaphoreType.DMA((3,)),
         ],
         compiler_params=pltpu.CompilerParams(vmem_limit_bytes=8 * 1024 * 1024),
     )(gram, turned, vectors, rotation)

time: 44.2 us -> 43.9 us (level)
  no operation moved by 1% of the time
where the time goes in v5:
time: 43.9 us; the launch traced here: 43.8 us
  Pallas kernels  43.1 us (98%)
  between operations  0.67 us (2%)
    pallas_call x1, Pallas kernels, local(): pl.pallas_call(functools.partial(kernel, n_wide, n_narrow, per_z, z_high)...  41.9 us
    pallas_call x1, Pallas kernels, local(): pl.pallas_call(finish, out_shape=(jax.ShapeDtypeStruct((plane, rows, V),...  1.13 us

profile of v5, /device:TPU:1, one launch (start us, length us, event | category | flops | bytes accessed | tf_op | source)
XLA Modules:
  0.0 43.8 jit_solution(414829123819984437)
XLA Ops:
  0.6 0.0 copy-start
  0.6 0.0 copy-start.1
  0.7 41.9 %shard_map.86 = (f32[32,8,128]{2,1,0:T(8,128)S(1)}, f32[2,384,128]{2,1,0:T(8,128)S(1)}) custom-call(bf16[3,128,128]{2,1,0:T(8,128)(2,1)} %vec_ref.1, bf16[3,3,61,128]{3,2,1,0:T(8,128)(2,1)} %hess_in.1, s32[60,128]{1,0:T(8,128)} %nbr_in.1, s32[1,32]{1,0:T(1,128)} %bitcast.3, s32[1,128]{1,0:T(1,128)} %bitcast.4, f32[2,16]{1,0:T(2,128)} %mass_in.1, ...), custom_call_target="tpu_custom_call" | custom-call | tf_op jit(solution)/shard_map/pallas_call | solution.py:415
  42.6 0.0 copy-done
  42.6 0.0 copy-done.1
  42.6 1.1 %shard_map.87 = (f32[32,8,128]{2,1,0:T(8,128)}, bf16[2,3,128,128]{3,2,1,0:T(8,128)(2,1)}) custom-call(f32[32,8,128]{2,1,0:T(8,128)S(1)} %get-tuple-element.6.gram_ref, f32[2,384,128]{2,1,0:T(8,128)S(1)} %get-tuple-element.7.turned_ref, bf16[3,128,128]{2,1,0:T(8,128)(2,1)S(1)} %copy-done.1, f32[2,128,128]{2,1,0:T(8,128)S(1)} %copy-done), custom_call_target="tpu_custom_call" | custom-call | tf_op jit(solution)/shard_map/pallas_call | solution.py:455
Async XLA Ops:
  0.6 42.0 %copy-start = (f32[2,128,128]{2,1,0:T(8,128)S(1)}, f32[2,128,128]{2,1,0:T(8,128)}, u32[]{:S(2)}) copy-start(f32[2,128,128]{2,1,0:T(8,128)} %rot_ref.1) | copy-start | bytes 393220
  0.6 42.0 %copy-start.1 = (bf16[3,128,128]{2,1,0:T(8,128)(2,1)S(1)}, bf16[3,128,128]{2,1,0:T(8,128)(2,1)}, u32[]{:S(2)}) copy-start(bf16[3,128,128]{2,1,0:T(8,128)(2,1)} %vec_ref.1) | copy-start | bytes 294916

commit v6 on v5

--- a/solution.py
+++ b/solution.py
@@ -17,7 +17,7 @@
 UNROLL = 30
 ROWS = A + 9 * H
 NISO = 16
-CORNERS, EDGES = (0, 2, 6, 8), (1, 3, 4, 5, 7)
+CORNERS, EDGES = (0, 6, 2, 8), (1, 3, 4, 5, 7)
 PAY = 3 * H + H // 2
 CENTRE = ROWS // 2
 
@@ -298,21 +298,23 @@
     for iso in range(2):
         scale = jnp.concatenate([all_factors[:, iso * V:(iso + 1) * V]] * 3, axis=1)
         high, low = split(corner_weights.astype(F32) * scale)
-        corner_left.append(split(dot(turned, high) + dot(turned, low)))
-
-    for name, copies in (("up", to_down), ("down", to_up)):
-        @pl.when(has[name])
-        def _():
-            copies[0].wait_recv()
-            copies[2].wait_recv()
-
-    corner_rows = far_rows(CORNERS)
+        left = split(dot(turned, high) + dot(turned, low))
+        corner_left.append([[part[:, :6 * H] for part in left], [part[:, 6 * H:] for part in left]])
+
+    grams = [first_gram[:, iso * V:(iso + 1) * V] for iso in range(2)]
+    corner_rows = []
+    for side in range(2):
+        for name, copies in (("up", to_down), ("down", to_up)):
+            pl.when(has[name])(copies[2 * side].wait_recv)
+        corner_rows.append(far_rows(CORNERS[2 * side:2 * side + 2]))
+        for iso in range(2):
+            high, low = corner_left[iso][side]
+            right = corner_rows[side][:, iso * V:(iso + 1) * V]
+            grams[iso] += dot(high, right) + dot(low, right)
+    corner_rows = jnp.concatenate(corner_rows, axis=0)
     rows = 2 * V // plane
     for iso in range(2):
-        high, low = corner_left[iso]
-        right = corner_rows[:, iso * V:(iso + 1) * V]
-        gram = first_gram[:, iso * V:(iso + 1) * V] + (dot(high, right) + dot(low, right))
-        g_ref[iso * (plane // 2):(iso + 1) * (plane // 2)] = gram.reshape(plane // 2, rows, V)
+        g_ref[iso * (plane // 2):(iso + 1) * (plane // 2)] = grams[iso].reshape(plane // 2, rows, V)
 
     def scatter(d):
         device, target = plane_device(d)

time: 43.9 us -> 44 us (level)
  no operation moved by 1% of the time
where the time goes in v6:
time: 44 us; the launch traced here: 43.9 us
  Pallas kernels  43.2 us (98%)
  between operations  0.67 us (2%)
    pallas_call x1, Pallas kernels, local(): pl.pallas_call(functools.partial(kernel, n_wide, n_narrow, per_z, z_high)...  42.1 us
    pallas_call x1, Pallas kernels, local(): pl.pallas_call(finish, out_shape=(jax.ShapeDtypeStruct((plane, rows, V),...  1.13 us

profile of v6, /device:TPU:1, one launch (start us, length us, event | category | flops | bytes accessed | tf_op | source)
XLA Modules:
  0.0 43.9 jit_solution(7815238802820206910)
XLA Ops:
  0.6 0.0 copy-start
  0.6 0.0 copy-start.1
  0.7 42.1 %shard_map.86 = (f32[32,8,128]{2,1,0:T(8,128)S(1)}, f32[2,384,128]{2,1,0:T(8,128)S(1)}) custom-call(bf16[3,128,128]{2,1,0:T(8,128)(2,1)} %vec_ref.1, bf16[3,3,61,128]{3,2,1,0:T(8,128)(2,1)} %hess_in.1, s32[60,128]{1,0:T(8,128)} %nbr_in.1, s32[1,32]{1,0:T(1,128)} %bitcast.3, s32[1,128]{1,0:T(1,128)} %bitcast.4, f32[2,16]{1,0:T(2,128)} %mass_in.1, ...), custom_call_target="tpu_custom_call" | custom-call | tf_op jit(solution)/shard_map/pallas_call | solution.py:417
  42.7 0.0 copy-done
  42.7 0.0 copy-done.1
  42.8 1.1 %shard_map.87 = (f32[32,8,128]{2,1,0:T(8,128)}, bf16[2,3,128,128]{3,2,1,0:T(8,128)(2,1)}) custom-call(f32[32,8,128]{2,1,0:T(8,128)S(1)} %get-tuple-element.6.gram_ref, f32[2,384,128]{2,1,0:T(8,128)S(1)} %get-tuple-element.7.turned_ref, bf16[3,128,128]{2,1,0:T(8,128)(2,1)S(1)} %copy-done.1, f32[2,128,128]{2,1,0:T(8,128)S(1)} %copy-done), custom_call_target="tpu_custom_call" | custom-call | tf_op jit(solution)/shard_map/pallas_call | solution.py:457
Async XLA Ops:
  0.6 42.1 %copy-start = (f32[2,128,128]{2,1,0:T(8,128)S(1)}, f32[2,128,128]{2,1,0:T(8,128)}, u32[]{:S(2)}) copy-start(f32[2,128,128]{2,1,0:T(8,128)} %rot_ref.1) | copy-start | bytes 393220
  0.6 42.1 %copy-start.1 = (bf16[3,128,128]{2,1,0:T(8,128)(2,1)S(1)}, bf16[3,128,128]{2,1,0:T(8,128)(2,1)}, u32[]{:S(2)}) copy-start(bf16[3,128,128]{2,1,0:T(8,128)(2,1)} %vec_ref.1) | copy-start | bytes 294916
